TPU v7x, 256 devices: a whole 4x4x8 slice. The times are simulated.
256 devices in a mesh: dom: 8 (over z), row: 16 (over y, x), col: 2 (over core).
Axes of the slice: x: 4, y: 4, z: 8, core: 2. Of those that a mesh axis runs over, the one named last changes fastest.
Arguments:
- next_inverse: bfloat16 [8, 4096, 4096], P('dom', 'row', 'col'), may hold values from -6 to 6
- next_arrow: bfloat16 [8, 64, 4096], P('dom', None, 'row'), may hold values from -6 to 6
- factor_win: bfloat16 [8, 4096, 3072], P('dom', 'row', 'col'), may hold values from -0.09375 to 0.09375
- factor_rest: bfloat16 [8, 4096, 1024], P('dom', 'row', 'col'), may hold values from -0.09375 to 0.09375
- arrow_win: bfloat16 [8, 64, 3072], P('dom', None, 'col'), may hold values from -0.75 to 0.75
- arrow_rest: bfloat16 [8, 64, 1024], P('dom', None, 'col'), may hold values from -0.75 to 0.75
- tip_inverse: bfloat16 [64, 64], replicated, may hold values from -6 to 6
- base_win: bfloat16 [8, 3072, 3072], P('dom', 'row', 'col'), may hold values from -6 to 6
- base_rest: bfloat16 [8, 3072, 1024], P('dom', 'row', 'col'), may hold values from -6 to 6
Outputs:
- sub_inverse: bfloat16 [8, 4096, 3072], P('dom', 'row', 'col')
- arrow_inverse: bfloat16 [8, 64, 3072], P('dom', None, 'col')
- diag_win: bfloat16 [8, 3072, 3072], P('dom', 'row', 'col')
- diag_rest: bfloat16 [8, 3072, 1024], P('dom', 'row', 'col')
All inputs are finite; a program needn't handle non-finite values.
Results may differ from a plain program's by a relative error of at most 0.0046.
Values may be sent and summed in bfloat16 or wider, within the bound.
A program may use at most 128 MiB of HBM per device.

v0:
```python
import jax
import jax.numpy as jnp
from jax import lax
from jax.sharding import PartitionSpec as P


def shifted(value, axis, steps):
    count = lax.axis_size(axis)
    leading, last = (max(0, -steps), min(count, count - steps))
    return lax.ppermute(value, axis, [(source, source + steps) for source in range(leading, last)])


def contract_first(left, right):
    return lax.dot_general(
        left, right, (((0,), (0,)), ((), ())), preferred_element_type=jnp.float32
    )


def per_device(
    next_inverse,
    next_arrow,
    factor_win,
    factor_rest,
    arrow_win,
    arrow_rest,
    tip_inverse,
    base_win,
    base_rest,
):
    inverse_tile = next_inverse[0]
    arrow_tile = next_arrow[0]
    factor_tile = factor_win[0]
    factor_other = factor_rest[0]
    ratio_tile = arrow_win[0]
    ratio_other = arrow_rest[0]
    factor_column = lax.all_gather(factor_tile, "row", axis=0, tiled=True)
    inverse_next, arrow_next = shifted((inverse_tile, arrow_tile), "dom", -1)
    start_sum = contract_first(arrow_next, ratio_tile)
    x_total = start_sum + jnp.dot(
        lax.all_gather(inverse_next, "col", axis=1, tiled=True),
        factor_column,
        preferred_element_type=jnp.float32,
    )
    x_bf = x_total.astype(jnp.bfloat16)
    y_part = jnp.dot(arrow_next, factor_tile, preferred_element_type=jnp.float32)
    y_total = lax.psum(y_part, "row") + jnp.dot(
        tip_inverse, ratio_tile, preferred_element_type=jnp.float32
    )
    y_bf = y_total.astype(jnp.bfloat16)
    x_panel, y_panel = (
        lax.all_gather(x_bf, "col", axis=1, tiled=True),
        lax.all_gather(y_bf, "col", axis=1, tiled=True),
    )
    ratio_both = jnp.concatenate([ratio_tile, ratio_other], axis=1)
    rows_here = y_panel.shape[1] // lax.axis_size("row")
    y_rows = lax.dynamic_slice_in_dim(y_panel, lax.axis_index("row") * rows_here, rows_here, 1)
    x_columns = lax.all_to_all(x_panel, "row", split_axis=1, concat_axis=0, tiled=True)
    rest_column = lax.all_gather(factor_other, "row", axis=0, tiled=True)
    factor_full = jnp.concatenate([factor_column, rest_column], axis=1)
    diag_part = contract_first(x_columns, factor_full)
    base_both = jnp.concatenate([base_win[0], base_rest[0]], axis=1).astype(jnp.float32)
    diag_total = base_both + diag_part + contract_first(y_rows, ratio_both)
    split = factor_tile.shape[1]
    diag_left = diag_total[:, :split].astype(jnp.bfloat16)
    diag_right = diag_total[:, split:].astype(jnp.bfloat16)
    return ((-x_bf)[None], (-y_bf)[None], diag_left[None], diag_right[None])


def solution(mesh):
    in_specs = (
        P("dom", "row", "col"),
        P("dom", None, "row"),
        P("dom", "row", "col"),
        P("dom", "row", "col"),
        P("dom", None, "col"),
        P("dom", None, "col"),
        P(),
        P("dom", "row", "col"),
        P("dom", "row", "col"),
    )
    out_specs = (
        P("dom", "row", "col"),
        P("dom", None, "col"),
        P("dom", "row", "col"),
        P("dom", "row", "col"),
    )
    return jax.shard_map(
        per_device, mesh=mesh, in_specs=in_specs, out_specs=out_specs, check_vma=False
    )
```

profile of v0, /device:TPU:1, one launch (start us, length us, event | category | flops | bytes accessed | tf_op | source)
XLA Modules:
  0.0 360.3 jit_solution(10407591954021950761)
XLA Ops:
  7.2 0.0 copy-start
  7.2 0.0 copy-start.7
  7.2 0.0 all-gather.7.cloned.1.call-start
  7.2 1.3 collective-permute-start.1
  8.5 24.2 %collective-permute-done.1 = bf16[256,2048]{1,0:T(8,128)(2,1)S(1)} collective-permute-done((bf16[256,2048]{1,0:T(8,128)(2,1)}, bf16[256,2048]{1,0:T(8,128)(2,1)S(1)}, u32[]{:S(2)}, u32[]{:S(2)}) %collective-permute-start.1) | collective-permute-done | bytes 1048608 | tf_op jit(solution)/shard_map/ppermute | solution.py:10
  32.8 0.0 copy-start.4
  32.8 1.0 copy-done.4
  33.8 0.0 all-gather.7.cloned.1.call-update
  33.8 0.0 all-gather.11.cloned.1.call-start
  33.9 0.7 all-gather.11.cloned.1.call-update
  34.6 0.0 all-gather.9.cloned.1.call-start
  34.6 0.0 copy-done.7
  34.6 0.0 copy-start.3
  34.6 1.4 collective-permute-start
  36.1 19.8 %all-gather.7.cloned.1.call-done = bf16[256,4096]{1,0:T(8,128)(2,1)} async-done(((bf16[256,2048]{1,0:T(8,128)(2,1)}), bf16[256,4096]{1,0:T(8,128)(2,1)}) %all-gather.7.cloned.1.call-update) | async-done | bytes 2097168 | tf_op jit(solution)/shard_map/all_gather | solution.py:40
  55.9 98.0 %all-gather.11.cloned.1.call-done = bf16[1,4096,1536]{2,1,0:T(8,128)(2,1)} async-done(((bf16[1,256,1536]{2,1,0:T(8,128)(2,1)}), bf16[1,4096,1536]{2,1,0:T(8,128)(2,1)}) %all-gather.11.cloned.1.call-update) | async-done | bytes 12582928 | tf_op jit(solution)/shard_map/all_gather | solution.py:36
  153.9 7.0 %fusion.18 = f32[256,1536]{1,0:T(8,128)S(1)} fusion(bf16[256,4096]{1,0:T(8,128)(2,1)} %all-gather.7.cloned.1.call-done, bf16[1,4096,1536]{2,1,0:T(8,128)(2,1)} %all-gather.11.cloned.1.call-done), kind=kOutput, calls=%fused_computation.23 | convolution fusion | flops 3221225472 | bytes 16252928 | tf_op jit(solution)/shard_map/dot_general | solution.py:39
  160.9 0.0 copy-start.2
  160.9 0.0 collective-permute-done
  161.0 0.0 copy-done.3
  161.0 1.3 fusion.4
  162.2 0.0 all-gather.9.cloned.1.call-update
  162.3 0.0 all-reduce.2.cloned.1.call-start
  162.3 0.0 copy-done.2
  162.3 1.0 fusion.9
  163.3 0.0 all-reduce.2.cloned.1.call-update
  163.3 0.0 all-gather.13.cloned.1.call-start
  163.4 0.5 all-gather.13.cloned.1.call-update
  163.9 14.1 %all-gather.9.cloned.1.call-done = bf16[256,3072]{1,0:T(8,128)(2,1)} async-done(((bf16[256,1536]{1,0:T(8,128)(2,1)}), bf16[256,3072]{1,0:T(8,128)(2,1)}) %all-gather.9.cloned.1.call-update) | async-done | bytes 1572880 | tf_op jit(solution)/shard_map/all_gather | solution.py:51
  178.0 2.6 copy.13
  180.6 6.3 %all-to-all-start = ((bf16[256,16,192]{0,2,1:T(8,128)(2,1)}), bf16[256,16,192]{0,2,1:T(8,128)(2,1)S(1)}, u32[]{:S(2)}, u32[]{:S(2)}) async-start(bf16[256,16,192]{0,2,1:T(8,128)(2,1)} %bitcast.9), calls=%async_computation | async-start | bytes 3145728 | tf_op jit(solution)/shard_map/all_to_all | solution.py:57
  186.9 0.0 copy-start.1
  186.9 0.0 copy-done
  186.9 0.2 fusion.20
  187.1 95.9 %all-reduce.2.cloned.1.call-done = f32[64,1536]{1,0:T(8,128)} async-done(((f32[64,1536]{1,0:T(8,128)}), f32[64,1536]{1,0:T(8,128)}) %all-reduce.2.cloned.1.call-update) | async-done | bytes 393232 | tf_op jit(solution)/shard_map/psum | solution.py:46
  283.0 1.7 negate_bitcast_fusion.1
  284.7 3.8 %all_gather.19 = bf16[64,3072]{1,0:T(8,128)(2,1)} all-gather(bf16[64,1536]{1,0:T(8,128)(2,1)S(1)} %get-tuple-element.5), channel_id=1, replica_groups=mesh['dom'=8,'row'=16,'col'=2] {'col'}, dimensions={1}, use_global_device_ids=true | all-gather | bytes 589824 | tf_op jit(solution)/shard_map/all_gather | solution.py:52
  288.5 0.0 copy-done.1
  288.5 0.9 negate_bitcast_fusion
  289.4 0.0 all-to-all-done
  289.4 0.2 copy.15
  289.6 53.0 %all-gather.13.cloned.1.call-done = bf16[1,4096,512]{2,1,0:T(8,128)(2,1)} async-done(((bf16[1,256,512]{2,1,0:T(8,128)(2,1)}), bf16[1,4096,512]{2,1,0:T(8,128)(2,1)}) %all-gather.13.cloned.1.call-update) | async-done | bytes 4194320 | tf_op jit(solution)/shard_map/all_gather | solution.py:58
  342.6 0.0 copy-done.6
  342.6 8.4 %fusion.5 = f32[192,2048]{1,0:T(8,128)S(1)} fusion(bf16[4096,192]{0,1:T(8,128)(2,1)S(1)} %bitcast.36, bf16[4096,512]{1,0:T(8,128)(2,1)} %bitcast.39, bf16[4096,1536]{1,0:T(8,128)(2,1)} %bitcast.38, bf16[192,512]{1,0:T(8,128)(2,1)S(1)} %bitcast.42, bf16[192,1536]{1,0:T(8,128)(2,1)} %bitcast.41), kind=kOutput, calls=%fused_computation.7 | convolution fusion | flops 3256745984 | bytes 20709376 | tf_op jit(solution)/shard_map/dot_general | solution.py:14
  350.9 0.0 copy-done.5
  351.0 1.3 fusion.8
  352.2 0.9 slice_bitcast_fusion
  353.1 0.7 slice_bitcast_fusion.1
  (2 shorter events, 0.0 us)
Async XLA Ops:
  7.2 179.7 %copy-start = (bf16[64,64]{1,0:T(8,128)(2,1)S(1)}, bf16[64,64]{1,0:T(8,128)(2,1)}, u32[]{:S(2)}) copy-start(bf16[64,64]{1,0:T(8,128)(2,1)} %param.15) | copy-start | bytes 24580
  7.2 27.4 %copy-start.7 = (bf16[1,64,256]{2,1,0:T(8,128)(2,1)S(1)}, bf16[1,64,256]{2,1,0:T(8,128)(2,1)}, u32[]{:S(2)}) copy-start(bf16[1,64,256]{2,1,0:T(8,128)(2,1)} %param.10) | copy-start | bytes 98308
  7.2 48.7 %all-gather.7.cloned.1.call-start = ((), (), s32[]{:S(2)}) async-start(), calls=%async_computation.1 | async-start | bytes 3145728 | tf_op jit(solution)/shard_map/all_gather | solution.py:40
  7.2 25.5 %collective-permute-start.1 = (bf16[256,2048]{1,0:T(8,128)(2,1)}, bf16[256,2048]{1,0:T(8,128)(2,1)S(1)}, u32[]{:S(2)}, u32[]{:S(2)}) collective-permute-start(bf16[256,2048]{1,0:T(8,128)(2,1)} %bitcast.40), channel_id=1, source_target_pairs={{32,0},{64,32},{96,64},{128,96},{160,128},{192,160},{224,192},{33,... | collective-permute-start | bytes 3145736 | tf_op jit(solution)/shard_map/ppermute | solution.py:10
  32.8 1.0 copy-start.4
  33.8 120.1 %all-gather.11.cloned.1.call-start = ((), (), s32[]{:S(2)}) async-start(), calls=%async_computation.4 | async-start | bytes 13369344 | tf_op jit(solution)/shard_map/all_gather | solution.py:36
  34.6 143.5 %all-gather.9.cloned.1.call-start = ((), (), s32[]{:S(2)}) async-start(), calls=%async_computation.3 | async-start | bytes 2359296 | tf_op jit(solution)/shard_map/all_gather | solution.py:51
  34.6 126.3 %copy-start.3 = (bf16[1,64,1536]{2,1,0:T(8,128)(2,1)S(1)}, bf16[1,64,1536]{2,1,0:T(8,128)(2,1)}, u32[]{:S(2)}) copy-start(bf16[1,64,1536]{2,1,0:T(8,128)(2,1)} %param.13) | copy-start | bytes 589828
  34.6 126.3 %collective-permute-start = (bf16[64,256]{1,0:T(8,128)(2,1)S(1)}, bf16[64,256]{1,0:T(8,128)(2,1)S(1)}, u32[]{:S(2)}, u32[]{:S(2)}) collective-permute-start(bf16[64,256]{1,0:T(8,128)(2,1)S(1)} %bitcast.43), channel_id=1, source_target_pairs={{32,0},{64,32},{96,64},{128,96},{160,128},{192,160},{224,192},{33,... | collective-permute-start | bytes 98312 | tf_op jit(solution)/shard_map/ppermute | solution.py:10
  160.9 1.4 copy-start.2
  162.3 120.7 %all-reduce.2.cloned.1.call-start = ((), (), s32[]{:S(2)}) async-start(), calls=%async_computation.2 | async-start | bytes 786432 | tf_op jit(solution)/shard_map/psum | solution.py:46
  163.3 179.2 %all-gather.13.cloned.1.call-start = ((), (), s32[]{:S(2)}) async-start(), calls=%async_computation.5 | async-start | bytes 4456448 | tf_op jit(solution)/shard_map/all_gather | solution.py:58
  180.6 108.8 %all-to-all-start = ((bf16[256,16,192]{0,2,1:T(8,128)(2,1)}), bf16[256,16,192]{0,2,1:T(8,128)(2,1)S(1)}, u32[]{:S(2)}, u32[]{:S(2)}) async-start(bf16[256,16,192]{0,2,1:T(8,128)(2,1)} %bitcast.9), calls=%async_computation | async-start | bytes 3145728 | tf_op jit(solution)/shard_map/all_to_all | solution.py:57
  186.9 101.6 %copy-start.1 = (bf16[256,1536]{1,0:T(8,128)(2,1)S(1)}, bf16[256,1536]{1,0:T(8,128)(2,1)}, u32[]{:S(2)}) copy-start(bf16[256,1536]{1,0:T(8,128)(2,1)} %fusion.4) | copy-start | bytes 2359300
  289.4 53.1 %copy-start.6 = (bf16[1,192,512]{2,1,0:T(8,128)(2,1)S(1)}, bf16[1,192,512]{2,1,0:T(8,128)(2,1)}, u32[]{:S(2)}) copy-start(bf16[1,192,512]{2,1,0:T(8,128)(2,1)} %param.17) | copy-start | bytes 589828
  342.6 8.4 %copy-start.5 = (bf16[1,64,512]{2,1,0:T(8,128)(2,1)S(1)}, bf16[1,64,512]{2,1,0:T(8,128)(2,1)}, u32[]{:S(2)}) copy-start(bf16[1,64,512]{2,1,0:T(8,128)(2,1)} %param.14) | copy-start | bytes 196612
Sparse Core Ops, SparseCore 0:
  33.9 21.8 all-gather.6
  58.3 95.5 all-gather.10
  162.4 15.6 all-gather.8
  181.7 101.2 all-reduce.1
  285.3 57.2 all-gather.12
where the time goes:
time: 361 us; the launch traced here: 360 us
  waiting for transfers between devices  306 us (85%)
  matrix products  19.1 us (5%)
  between operations  13.9 us (4%)
  starting transfers between devices  9.18 us (3%)
  local copies, waits for them, and re-layouts  5.35 us (1%)
  blocking collectives  3.8 us (1%)
    all_gather x1, waiting for transfers between devices, per_device(): factor_column = lax.all_gather(factor_tile, 'row', axis=0, tiled=True)  98 us
    psum x1, waiting for transfers between devices, per_device(): lax.psum(y_part, 'row')  95.9 us
    all_gather x1, waiting for transfers between devices, per_device(): rest_column = lax.all_gather(factor_other, 'row', axis=0, tiled=True)  53 us
    ppermute x2, waiting for transfers between devices, shifted(): lax.ppermute(value, axis, [(source, source + steps) for source in range(l...  24.2 us
    all_gather x1, waiting for transfers between devices, per_device(): lax.all_gather(inverse_next, 'col', axis=1, tiled=True)  19.8 us
    all_gather x1, waiting for transfers between devices, per_device(): lax.all_gather(x_bf, 'col', axis=1, tiled=True)  14.1 us
    dot_general x3, matrix products, contract_first(): lax.dot_general(left, right, (((0,), (0,)), ((), ())), preferred_element_...  10.9 us
  transfers between devices with their start and end apart: 8, of which 6 were waited for; matrix products, arithmetic and copies ran while one was open for 4% of the time, Pallas kernels for 0%

commit v1 on v0

--- a/solution.py
+++ b/solution.py
@@ -43,7 +43,7 @@
     )
     x_bf = x_total.astype(jnp.bfloat16)
     y_part = jnp.dot(arrow_next, factor_tile, preferred_element_type=jnp.float32)
-    y_total = lax.psum(y_part, "row") + jnp.dot(
+    y_total = jnp.sum(lax.all_gather(y_part, "row"), axis=0) + jnp.dot(
         tip_inverse, ratio_tile, preferred_element_type=jnp.float32
     )
     y_bf = y_total.astype(jnp.bfloat16)

time: 361 us -> 334 us (0.925)
  waiting for transfers between devices: 306 us -> 278 us
    psum x1 -> x0, waiting for transfers between devices: 95.9 us -> none  [per_device(): lax.psum(y_part, 'row')]
    all_gather x0 -> x1, waiting for transfers between devices: none -> 70.2 us  [per_device(): lax.all_gather(y_part, 'row')]
  transfers between devices with their start and end apart: 8 -> 8, of which waited for: 6 -> 6; matrix products, arithmetic and copies ran while one was open for 4% -> 5% of each run, Pallas kernels for 0% -> 0%
where the time goes in v1:
time: 334 us
  waiting for transfers between devices  278 us (83%)
  matrix products  19.1 us (6%)
  between operations  13.9 us (4%)
  starting transfers between devices  9.18 us (3%)
  local copies, waits for them, and re-layouts  5.39 us (2%)
  other arithmetic  4.83 us (1%)
    all_gather x1, waiting for transfers between devices, per_device(): factor_column = lax.all_gather(factor_tile, 'row', axis=0, tiled=True)  98 us
    all_gather x1, waiting for transfers between devices, per_device(): lax.all_gather(y_part, 'row')  70.2 us
    all_gather x1, waiting for transfers between devices, per_device(): rest_column = lax.all_gather(factor_other, 'row', axis=0, tiled=True)  50.7 us
    ppermute x2, waiting for transfers between devices, shifted(): lax.ppermute(value, axis, [(source, source + steps) for source in range(l...  24.2 us
    all_gather x1, waiting for transfers between devices, per_device(): lax.all_gather(inverse_next, 'col', axis=1, tiled=True)  19.8 us
    all_gather x1, waiting for transfers between devices, per_device(): lax.all_gather(x_bf, 'col', axis=1, tiled=True)  14.1 us
    dot_general x3, matrix products, contract_first(): lax.dot_general(left, right, (((0,), (0,)), ((), ())), preferred_element_...  10.9 us
    dot_general x1, matrix products, per_device(): jnp.dot(lax.all_gather(inverse_next, 'col', axis=1, tiled=True), factor_c...  7.04 us
  transfers between devices with their start and end apart: 8, of which 6 were waited for; matrix products, arithmetic and copies ran while one was open for 5% of the time, Pallas kernels for 0%

profile of v1, /device:TPU:1, one launch (start us, length us, event | category | flops | bytes accessed | tf_op | source)
XLA Modules:
  0.0 333.5 jit_solution(8709053575254865340)
XLA Ops:
  7.2 0.0 copy-start
  7.2 0.0 copy-start.7
  7.2 0.0 all-gather.9.cloned.1.call-start
  7.2 1.3 collective-permute-start.1
  8.5 24.2 %collective-permute-done.1 = bf16[256,2048]{1,0:T(8,128)(2,1)S(1)} collective-permute-done((bf16[256,2048]{1,0:T(8,128)(2,1)}, bf16[256,2048]{1,0:T(8,128)(2,1)S(1)}, u32[]{:S(2)}, u32[]{:S(2)}) %collective-permute-start.1) | collective-permute-done | bytes 1048608 | tf_op jit(solution)/shard_map/ppermute | solution.py:10
  32.8 1.0 copy-done.4
  33.8 0.0 all-gather.9.cloned.1.call-update
  33.8 0.0 all-gather.13.cloned.1.call-start
  33.8 0.7 all-gather.13.cloned.1.call-update
  34.5 0.0 all-gather.11.cloned.1.call-start
  34.6 0.0 copy-done.7
  34.6 0.0 copy-start.3
  34.6 1.4 collective-permute-start
  36.0 19.8 %all-gather.9.cloned.1.call-done = bf16[256,4096]{1,0:T(8,128)(2,1)} async-done(((bf16[256,2048]{1,0:T(8,128)(2,1)}), bf16[256,4096]{1,0:T(8,128)(2,1)}) %all-gather.9.cloned.1.call-update) | async-done | bytes 2097168 | tf_op jit(solution)/shard_map/all_gather | solution.py:40
  55.9 98.0 %all-gather.13.cloned.1.call-done = bf16[1,4096,1536]{2,1,0:T(8,128)(2,1)} async-done(((bf16[1,256,1536]{2,1,0:T(8,128)(2,1)}), bf16[1,4096,1536]{2,1,0:T(8,128)(2,1)}) %all-gather.13.cloned.1.call-update) | async-done | bytes 12582928 | tf_op jit(solution)/shard_map/all_gather | solution.py:36
  153.9 7.0 %fusion.19 = f32[256,1536]{1,0:T(8,128)S(1)} fusion(bf16[256,4096]{1,0:T(8,128)(2,1)} %all-gather.9.cloned.1.call-done, bf16[1,4096,1536]{2,1,0:T(8,128)(2,1)} %all-gather.13.cloned.1.call-done), kind=kOutput, calls=%fused_computation.24 | convolution fusion | flops 3221225472 | bytes 16252928 | tf_op jit(solution)/shard_map/dot_general | solution.py:39
  160.9 0.0 copy-start.2
  161.0 0.0 collective-permute-done
  161.0 0.0 copy-done.3
  161.0 1.3 fusion.4
  162.2 0.0 all-gather.11.cloned.1.call-update
  162.3 0.0 all-gather.15.cloned.1.call-start
  162.3 0.0 copy-done.2
  162.3 1.0 fusion.10
  163.3 0.0 all-gather.15.cloned.1.call-update
  163.4 0.0 all-gather.17.cloned.1.call-start
  163.4 0.5 all-gather.17.cloned.1.call-update
  163.9 14.1 %all-gather.11.cloned.1.call-done = bf16[256,3072]{1,0:T(8,128)(2,1)} async-done(((bf16[256,1536]{1,0:T(8,128)(2,1)}), bf16[256,3072]{1,0:T(8,128)(2,1)}) %all-gather.11.cloned.1.call-update) | async-done | bytes 1572880 | tf_op jit(solution)/shard_map/all_gather | solution.py:51
  178.0 2.6 copy.13
  180.7 6.3 %all-to-all-start = ((bf16[256,16,192]{0,2,1:T(8,128)(2,1)}), bf16[256,16,192]{0,2,1:T(8,128)(2,1)S(1)}, u32[]{:S(2)}, u32[]{:S(2)}) async-start(bf16[256,16,192]{0,2,1:T(8,128)(2,1)} %bitcast.10), calls=%async_computation | async-start | bytes 3145728 | tf_op jit(solution)/shard_map/all_to_all | solution.py:57
  186.9 70.2 %all-gather.15.cloned.1.call-done = f32[1024,1536]{1,0:T(8,128)} async-done(((f32[64,1536]{1,0:T(8,128)}), f32[1024,1536]{1,0:T(8,128)}) %all-gather.15.cloned.1.call-update) | async-done | bytes 6291472 | tf_op jit(solution)/shard_map/all_gather | solution.py:46
  257.2 3.2 reduce_sum.9
  260.4 0.0 copy-done
  260.4 0.0 copy-start.1
  260.4 0.2 fusion.9
  260.6 2.7 all_gather.27
  263.2 0.7 negate_bitcast_fusion.1
  263.9 0.0 copy-done.1
  263.9 0.9 negate_bitcast_fusion
  264.9 0.0 all-to-all-done
  264.9 0.2 copy.15
  265.0 50.7 %all-gather.17.cloned.1.call-done = bf16[1,4096,512]{2,1,0:T(8,128)(2,1)} async-done(((bf16[1,256,512]{2,1,0:T(8,128)(2,1)}), bf16[1,4096,512]{2,1,0:T(8,128)(2,1)}) %all-gather.17.cloned.1.call-update) | async-done | bytes 4194320 | tf_op jit(solution)/shard_map/all_gather | solution.py:58
  315.8 0.0 copy-done.6
  315.8 8.4 %fusion.5 = f32[192,2048]{1,0:T(8,128)S(1)} fusion(bf16[4096,192]{0,1:T(8,128)(2,1)S(1)} %bitcast.38, bf16[4096,512]{1,0:T(8,128)(2,1)} %bitcast.41, bf16[4096,1536]{1,0:T(8,128)(2,1)} %bitcast.40, bf16[192,512]{1,0:T(8,128)(2,1)S(1)} %bitcast.44, bf16[192,1536]{1,0:T(8,128)(2,1)} %bitcast.43), kind=kOutput, calls=%fused_computation.7 | convolution fusion | flops 3256745984 | bytes 20709376 | tf_op jit(solution)/shard_map/dot_general | solution.py:14
  324.1 0.0 copy-done.5
  324.1 1.3 fusion.8
  325.4 0.9 slice_bitcast_fusion
  326.3 0.7 slice_bitcast_fusion.1
  (3 shorter events, 0.0 us)
Async XLA Ops:
  7.2 253.2 %copy-start = (bf16[64,64]{1,0:T(8,128)(2,1)S(1)}, bf16[64,64]{1,0:T(8,128)(2,1)}, u32[]{:S(2)}) copy-start(bf16[64,64]{1,0:T(8,128)(2,1)} %param.15) | copy-start | bytes 24580
  7.2 27.4 %copy-start.7 = (bf16[1,64,256]{2,1,0:T(8,128)(2,1)S(1)}, bf16[1,64,256]{2,1,0:T(8,128)(2,1)}, u32[]{:S(2)}) copy-start(bf16[1,64,256]{2,1,0:T(8,128)(2,1)} %param.10) | copy-start | bytes 98308
  7.2 48.7 %all-gather.9.cloned.1.call-start = ((), (), s32[]{:S(2)}) async-start(), calls=%async_computation.1 | async-start | bytes 3145728 | tf_op jit(solution)/shard_map/all_gather | solution.py:40
  7.2 25.5 %collective-permute-start.1 = (bf16[256,2048]{1,0:T(8,128)(2,1)}, bf16[256,2048]{1,0:T(8,128)(2,1)S(1)}, u32[]{:S(2)}, u32[]{:S(2)}) collective-permute-start(bf16[256,2048]{1,0:T(8,128)(2,1)} %bitcast.42), channel_id=1, source_target_pairs={{32,0},{64,32},{96,64},{128,96},{160,128},{192,160},{224,192},{33,... | collective-permute-start | bytes 3145736 | tf_op jit(solution)/shard_map/ppermute | solution.py:10
  32.8 1.0 copy-start.4
  33.8 120.1 %all-gather.13.cloned.1.call-start = ((), (), s32[]{:S(2)}) async-start(), calls=%async_computation.3 | async-start | bytes 13369344 | tf_op jit(solution)/shard_map/all_gather | solution.py:36
  34.5 143.5 %all-gather.11.cloned.1.call-start = ((), (), s32[]{:S(2)}) async-start(), calls=%async_computation.2 | async-start | bytes 2359296 | tf_op jit(solution)/shard_map/all_gather | solution.py:51
  34.6 126.4 %copy-start.3 = (bf16[1,64,1536]{2,1,0:T(8,128)(2,1)S(1)}, bf16[1,64,1536]{2,1,0:T(8,128)(2,1)}, u32[]{:S(2)}) copy-start(bf16[1,64,1536]{2,1,0:T(8,128)(2,1)} %param.13) | copy-start | bytes 589828
  34.6 126.3 %collective-permute-start = (bf16[64,256]{1,0:T(8,128)(2,1)S(1)}, bf16[64,256]{1,0:T(8,128)(2,1)S(1)}, u32[]{:S(2)}, u32[]{:S(2)}) collective-permute-start(bf16[64,256]{1,0:T(8,128)(2,1)S(1)} %bitcast.45), channel_id=1, source_target_pairs={{32,0},{64,32},{96,64},{128,96},{160,128},{192,160},{224,192},{33,... | collective-permute-start | bytes 98312 | tf_op jit(solution)/shard_map/ppermute | solution.py:10
  160.9 1.4 copy-start.2
  162.3 94.9 %all-gather.15.cloned.1.call-start = ((), (), s32[]{:S(2)}) async-start(), calls=%async_computation.4 | async-start | bytes 6684672 | tf_op jit(solution)/shard_map/all_gather | solution.py:46
  163.4 152.4 %all-gather.17.cloned.1.call-start = ((), (), s32[]{:S(2)}) async-start(), calls=%async_computation.5 | async-start | bytes 4456448 | tf_op jit(solution)/shard_map/all_gather | solution.py:58
  180.7 84.2 %all-to-all-start = ((bf16[256,16,192]{0,2,1:T(8,128)(2,1)}), bf16[256,16,192]{0,2,1:T(8,128)(2,1)S(1)}, u32[]{:S(2)}, u32[]{:S(2)}) async-start(bf16[256,16,192]{0,2,1:T(8,128)(2,1)} %bitcast.10), calls=%async_computation | async-start | bytes 3145728 | tf_op jit(solution)/shard_map/all_to_all | solution.py:57
  260.4 3.5 %copy-start.1 = (bf16[256,1536]{1,0:T(8,128)(2,1)S(1)}, bf16[256,1536]{1,0:T(8,128)(2,1)}, u32[]{:S(2)}) copy-start(bf16[256,1536]{1,0:T(8,128)(2,1)} %fusion.4) | copy-start | bytes 2359300
  264.9 50.9 %copy-start.6 = (bf16[1,192,512]{2,1,0:T(8,128)(2,1)S(1)}, bf16[1,192,512]{2,1,0:T(8,128)(2,1)}, u32[]{:S(2)}) copy-start(bf16[1,192,512]{2,1,0:T(8,128)(2,1)} %param.17) | copy-start | bytes 589828
  315.8 8.4 %copy-start.5 = (bf16[1,64,512]{2,1,0:T(8,128)(2,1)S(1)}, bf16[1,64,512]{2,1,0:T(8,128)(2,1)}, u32[]{:S(2)}) copy-start(bf16[1,64,512]{2,1,0:T(8,128)(2,1)} %param.14) | copy-start | bytes 196612
Sparse Core Ops, SparseCore 0:
  33.9 21.8 all-gather.8
  58.3 95.5 all-gather.12
  162.4 15.5 all-gather.10
  180.9 76.2 all-gather.14
  259.4 56.2 all-gather.16
